TPU v7x, 128 devices: a whole 4x4x4 slice. The times are simulated.
128 devices in a mesh: row: 8 (over y, x_lo), col: 16 (over x_hi, z, core).
Axes of the slice: x: 4 (x_hi: 2, x_lo: 2; x = x_hi * 2 + x_lo), y: 4, z: 4, core: 2. Of those that a mesh axis runs over, the one named last changes fastest.
Arguments:
- front: float32 [16384, 16384], P('row', 'col'), may hold values from -6 to 6
- contrib: float32 [8192, 16384], P('row', 'col'), may hold values from -6 to 6
- pivot_inverse: float32 [4, 256, 256], replicated, may hold values from -0.0234375 to 0.0234375
- index_map: int32 [2, 32], replicated, may hold values from 0 to 63, as said below
- fill_mask: int32 [64, 64], replicated, may hold values from 0 to 1, as said below
Outputs:
- factored: float32 [16384, 16384], P('row', 'col')
Inputs may be any that keep to these rules, and one draw needn't show every extreme that they name: For each child h, index_map[h, a] = a + t_h(floor(a / 8)), where t_h is nondecreasing, t_h(0) <= 8 and t_h grows by at most 8 from one group to the next. For one of the two children, drawn from the seed, t_h(g) = (g + 1) * 8 for every group g. Hence every parent process row owns exactly 4 of a child's block indices, and the 4 consecutive child block columns held by one device land on distinct parent process columns. 1 marks a block of the fill pattern. It contains every block (index_map[h, a], index_map[h, b]) and is closed under the first 4 steps: for k < 4, i > k, j > k, fill_mask[i, k] = fill_mask[k, j] = 1 implies fill_mask[i, j] = 1.
All inputs are finite; a program needn't handle non-finite values.
Results may differ from a plain program's by a relative error of at most 0.00021.
Values sent between devices are 32-bit elements; how exact they have to be, the bound alone decides.
A program may use at most 192 MiB of HBM per device.

v0:
```python
import functools

import jax
import jax.numpy as jnp
from jax import lax
from jax.experimental import pallas as pl
from jax.experimental.pallas import tpu as pltpu
from jax.sharding import PartitionSpec as P

BS = 256
K = 4
WINDOW = 8
MESH = pl.DeviceIdType.MESH
f32 = jnp.float32
bf16 = jnp.bfloat16


def place(imap, child, g, h, z, core):
    t = imap[child, 8 * g] - 8 * g
    first = (core + t) % 2
    start = (4 * g + (t + first) // 2) % 8
    m = (z + 8 - start) % 4
    half = ((start + m) % 8) // 4
    block = 8 * g + t + first + 2 * m
    return half == h, block // 16


def local_row(imap, child, jj, r):
    t = imap[child, 8 * jj] - 8 * jj
    return jj + (t + (r + 64 - t) % 8) // 8


def exchange_kernel(
    free, imap, mask, contrib, front, pinv_hbm,
    R, X, LR, Vh_out, Vl_out, frow_out,
    UR, CR, PB, U, pinv, Vh, Vl, frow, ldp, outs,
    cv, SP, M0, M1, M2, M3, S, PC, PR, FC, FR, RB, RC,
    ld, ldf, cs, cr, zs, zr, xs, xr, own,
    ldb, ldc, lcopy, Ls, Lr, Lxs, Lcs, Lcr, L3s,
    Us, Ur, Ups, ucopy, Cs, Cr, Cps, ccopy, Ccs, Ccr,
):
    M = [M0, M1, M2, M3]
    r = lax.axis_index("row")
    c = lax.axis_index("col")
    y, e = r // 2, r % 2
    h, z, core = c // 8, (c // 2) % 4, c % 2

    def dev(y_, e_, h_, z_, core_):
        return (2 * y_ + e_, 8 * h_ + 2 * z_ + core_)

    core_peer = dev(y, e, h, z, 1 - core)
    x_peer = dev(y, e, 1 - h, z, core)
    e_peer = dev(y, 1 - e, h, z, core)

    def z_peer(z_):
        return dev(y, e, h, z_, core)

    def y_peer(y_):
        return dev(y_, e, h, z, core)

    def remote(src, dst, ss, rs, to):
        return pltpu.make_async_remote_copy(
            src_ref=src, dst_ref=dst, send_sem=ss, recv_sem=rs, device_id=to, device_id_type=MESH
        )

    def load_c(jj):
        return pltpu.make_async_copy(contrib.at[pl.ds(jj * BS, BS)], cv.at[jj], ld.at[jj])

    for jj in range(4):
        load_c(jj).start()
    never = jnp.bool_(False)
    is_col_source = (h == 0) & (z < 2)
    is_row_source = r < 4
    load_pinv = pltpu.make_async_copy(pinv_hbm, pinv, ldp.at[0])
    load_pinv.start()
    load_fc = pltpu.make_async_copy(front.at[:, pl.ds(0, BS)], FC, ldf.at[0])
    load_fr = pltpu.make_async_copy(front.at[pl.ds(0, BS)], FR, ldf.at[1])

    @pl.when(is_col_source)
    def _():
        load_fc.start()

    @pl.when(is_row_source)
    def _():
        load_fr.start()

    barrier = pltpu.get_barrier_semaphore()
    peers = [core_peer, x_peer, e_peer]
    peers += [z_peer((z + d) % 4) for d in (1, 2, 3)]
    peers += [y_peer((y + d) % 4) for d in (1, 3)]
    for p in peers:
        pl.semaphore_signal(barrier, inc=1, device_id=p, device_id_type=MESH)
    pl.semaphore_wait(barrier, len(peers))

    t_own = imap[h, 8 * z] - 8 * z
    odd_mine = (core + t_own) % 2
    start_own = (4 * z + (t_own + odd_mine) // 2) % 8

    def core_copy(jj):
        return remote(SP.at[jj], M[jj].at[pl.ds(2 * core, 2)], cs.at[jj], cr.at[jj], core_peer)

    def z_copy(jj, d):
        to = (z + d) % 4
        return remote(S.at[jj, to], R.at[z, jj], zs.at[jj, d], zr.at[jj, z], z_peer(to))

    def z_wait(jj, g):
        remote(S.at[jj, 0], R.at[g, jj], zs.at[jj, 0], zr.at[jj, g], z_peer(g)).wait_recv()

    def own_copy(jj):
        return pltpu.make_async_copy(S.at[jj, z], R.at[z, jj], own.at[jj])

    def x_own(jj):
        return remote(S.at[jj, z], X.at[z, jj], xs.at[jj, z], xr.at[jj, z], x_peer)

    def x_copy(jj, g):
        return remote(R.at[g, jj], X.at[g, jj], xs.at[jj, g], xr.at[jj, g], x_peer)

    queue = []

    def cross(jj, g):
        group = (z + g) % 4 if free else g
        if len(queue) >= WINDOW:
            x_copy(*queue[len(queue) - WINDOW]).wait_send()
        queue.append((jj, group))
        if free and g == 0:
            x_own(jj).start()
            return
        if free:
            z_wait(jj, group)
            x_copy(jj, group).start()
            return

        @pl.when(z != group)
        def _():
            z_wait(jj, group)
            x_copy(jj, group).start()

        @pl.when(z == group)
        def _():
            x_own(jj).start()

    def swap_cores():
        for jj in range(4):
            load_c(jj).wait()
            for i in range(2):
                even = cv[jj, :, 2 * i * BS:(2 * i + 1) * BS]
                odd = cv[jj, :, (2 * i + 1) * BS:(2 * i + 2) * BS]
                SP[jj, i] = jnp.where(odd_mine == 1, even, odd)
                M[jj][2 * core + i] = jnp.where(odd_mine == 1, odd, even)
            core_copy(jj).start()

    def arrange(jj):
        core_copy(jj).wait_recv()
        for to in range(4):
            S[jj, to] = M[jj][(to + 8 - start_own) % 4]
        own_copy(jj).start()

    def z_send(jj):
        for d in (1, 3, 2):
            z_copy(jj, d).start()

    def z_send_first(jj):
        @pl.when(z == 0)
        def _():
            z_copy(jj, 1).start()

    def z_send_rest(jj):
        @pl.when(z != 0)
        def _():
            z_copy(jj, 1).start()

        for d in (3, 2):
            z_copy(jj, d).start()

    def own_waits():
        for jj in range(4):
            own_copy(jj).wait()

    def y_next(way):
        return y_peer((y + (1 if way == 0 else 3)) % 4)

    def u_rows(way, q):
        return pl.ds(way * 128 + q * 64, 64)

    def u_copy(k, way, q, src):
        return remote(
            src, UR.at[k, u_rows(way, q)], Us.at[k, way, q], Ur.at[k, way, q], y_next(way)
        )

    def u_held(k, way, q):
        return UR.at[k, u_rows(way, q)]

    def u_partner(way, q):
        return remote(
            PR.at[u_rows(way, q)], UR.at[r, u_rows(way, q)],
            Ups.at[way, q], Ur.at[r, way, q], e_peer,
        )

    own_u = pltpu.make_async_copy(PR, UR.at[jnp.minimum(r, 3)], ucopy.at[0])

    def send_row_panel():
        own_u.start()
        for q in range(2):
            for way in range(2):
                u_partner(way, q).start()
                u_copy(r, way, q, PR.at[u_rows(way, q)]).start()

    def load_rb(w, g):
        return pltpu.make_async_copy((R, X)[w].at[g, 0], RB.at[w, g], ldb.at[w, g])

    def make_row_panel():
        @pl.when(is_row_source)
        def _():
            for g in range(4):
                load_rb(0, g).start()
            for g in range(4):
                if g == 0:
                    @pl.when(jnp.logical_not(is_col_source))
                    def _():
                        x_copy(0, 0).wait_recv()
                else:
                    x_copy(0, g).wait_recv()
                load_rb(1, g).start()
            load_fr.wait()
            for w in range(2):
                for g in range(4):
                    load_rb(w, g).wait()
            hit = []
            for w, child in enumerate((h, 1 - h)):
                row_in = local_row(imap, child, 0, r) == 0
                for g in range(4):
                    lands, at = place(imap, child, g, h, z, core)
                    hit.append((w, g, lands & row_in, at))
            for lc in range(4):
                weights = [
                    (w, g, jnp.where(ok & (at == lc), 1.0, 0.0).astype(f32)) for w, g, ok, at in hit
                ]
                present = mask[r, c + 16 * lc].astype(f32)

                @pl.loop(0, 8)
                def _(q):
                    rows = pl.ds(pl.multiple_of(q * 32, 32), 32)
                    total = FR[rows, lc * BS:(lc + 1) * BS]
                    for w, g, weight in weights:
                        total = total + weight * RB[w, g, rows, :]
                    PR[rows, lc * BS:(lc + 1) * BS] = total * present
            send_row_panel()

    def make_row_panel_free():
        @pl.when(is_row_source)
        def _():
            load_fr.wait()
            for lc in range(4):
                PR[:, lc * BS:(lc + 1) * BS] = (
                    FR[:, lc * BS:(lc + 1) * BS] * mask[r, c + 16 * lc].astype(f32)
                )
            send_row_panel()

    panel = 2 * z + core

    def l_next(l):
        return z_peer((z + (1 if l % 2 == 0 else 3)) % 4)

    def l_copy(s, l, src):
        return remote(src, LR.at[2 * s + core, l], Ls.at[s, l], Lr.at[s, l], l_next(l))

    def l_wait(s, l):
        l_copy(s, l, LR.at[2 * s + core, l]).wait_recv()

    def l_x(s, l):
        return remote(
            LR.at[2 * s + core, l], LR.at[2 * s + core, l], Lxs.at[s, l], Lr.at[s, l], x_peer
        )

    def l_x_source(l):
        return remote(PC.at[l], LR.at[panel, l], Lxs.at[z, l], Lr.at[z, l], x_peer)

    def l_core(s, l):
        return remote(
            LR.at[2 * s + core, l], LR.at[2 * s + core, l], Lcs.at[s, l], Lcr.at[s, l], core_peer
        )

    def l_three(s, l, d):
        return remote(
            LR.at[2 * s + core, l], LR.at[2 * s + core, l],
            L3s.at[s, l, d], Lr.at[s, l], z_peer((z + d) % 4),
        )

    shift = [0, 0, 2, 2, 1, 3, 1, 3]
    own_l = pltpu.make_async_copy(PC, LR.at[jnp.minimum(panel, 3)], lcopy.at[0])

    def send_column_block(l, value):
        PC[l] = value
        l_copy(z, l, PC.at[l]).start()
        if shift[l] == 0:
            l_x_source(l).start()

    def make_column_panel():
        @pl.when(is_col_source)
        def _():
            for jj in range(4):
                x_copy(jj, 0).wait_recv()
            loads = [pltpu.make_async_copy((R, X)[w].at[0], RC.at[w], ldc.at[w]) for w in range(2)]
            for load in loads:
                load.start()
            load_fc.wait()
            for load in loads:
                load.wait()
            hits = [place(imap, child, 0, h, z, core) for child in (h, 1 - h)]
            rows_at = [[local_row(imap, child, jj, r) for jj in range(4)] for child in (h, 1 - h)]
            for l in range(8):
                present = mask[r + 8 * l, c].astype(f32)
                total = FC[l * BS:(l + 1) * BS, :]
                for w in range(2):
                    lands, lc = hits[w]
                    index = jnp.int32(0)
                    found = jnp.int32(0)
                    for jj in range(4):
                        here = (rows_at[w][jj] == l).astype(jnp.int32)
                        index = jnp.where(here > 0, jj, index)
                        found = found + here
                    weight = jnp.where(lands & (lc == 0) & (found > 0), 1.0, 0.0).astype(f32)
                    total = total + weight * RC[w, index]
                send_column_block(l, total * present)
            own_l.start()

    def make_column_panel_free():
        @pl.when(is_col_source)
        def _():
            load_fc.wait()
            for l in range(8):
                send_column_block(l, FC[l * BS:(l + 1) * BS, :] * mask[r + 8 * l, c].astype(f32))
            own_l.start()

    def own_l_wait():
        @pl.when(is_col_source)
        def _():
            own_l.wait()

    def column_ring(step):
        for i in range(4):
            if not 1 <= step - i <= 3:
                continue
            for way in range(2):
                l = 2 * i + way
                for s in range(2):
                    dist = (z + 4 - s) % 4 if way == 0 else (s + 4 - z) % 4

                    @pl.when(dist == step - i)
                    def _():
                        l_wait(s, l)
                        if step - i < 3:
                            l_copy(s, l, LR.at[2 * s + core, l]).start()
                        if shift[l] != 0:
                            @pl.when(z == (s + shift[l]) % 4)
                            def _():
                                l_x(s, l).start()

                        l_core(s, l).start()

    def column_spread(l):
        for s in range(2):
            @pl.when(z == (s + shift[l]) % 4)
            def _():
                l_wait(s, l)
                for d in (1, 3, 2):
                    l_three(s, l, d).start()
                l_core(s, l).start()

    def column_rest(l):
        for s in range(2):
            @pl.when(z != (s + shift[l]) % 4)
            def _():
                l_wait(s, l)
                l_core(s, l).start()

    def column_slot(slot):
        @pl.when(h == 0)
        def _():
            if slot == 1:
                own_l_wait()
                for l in range(8):
                    @pl.when(z < 2)
                    def _():
                        l_core(z, l).start()

            column_ring(slot)
            if slot == 3:
                corner_start()

        @pl.when(h == 1)
        def _():
            if slot == 1:
                column_spread(0)
                column_spread(1)
            if slot == 2:
                column_rest(0)
                corner_start()
            if slot == 3:
                column_rest(1)
            if slot == 4:
                for l in (2, 3, 4, 5):
                    column_spread(l)
            if slot == 5:
                column_spread(6)
                column_spread(7)
                for l in (2, 3, 4, 5):
                    column_rest(l)
            if slot == 6:
                column_rest(6)
                column_rest(7)

    def c_held(k, s, q):
        return CR.at[k, core, s, pl.ds(128 * q, 128)]

    def c_from(s, q):
        return LR.at[2 * s + core, 0, pl.ds(128 * q, 128)]

    def c_copy(k, s, q, src):
        return remote(src, c_held(k, s, q), Cs.at[k, s, q], Cr.at[k, s, q], y_next(s))

    def c_partner(s, q):
        return remote(c_from(s, q), c_held(r, s, q), Cps.at[s, q], Cr.at[r, s, q], e_peer)

    def c_own(s):
        return pltpu.make_async_copy(
            LR.at[2 * s + core, 0], CR.at[jnp.minimum(r, 3), core, s], ccopy.at[s]
        )

    def c_core(k):
        return remote(CR.at[k, core], CR.at[k, core], Ccs.at[k], Ccr.at[k], core_peer)

    def ring_dist(k, way):
        s = k // 2
        return (y + 4 - s) % 4 if way == 0 else (s + 4 - y) % 4

    def row_ring(step):
        for q in range(2):
            if not 0 <= step - q <= 3:
                continue
            for k in range(4):
                for way in range(2):
                    @pl.when((r != k) & (ring_dist(k, way) == step - q))
                    def _():
                        u_copy(k, way, q, u_held(k, way, q)).wait_recv()
                        if step - q < 3:
                            u_copy(k, way, q, u_held(k, way, q)).start()

    def corner_ring(step):
        for q in range(2):
            if not 0 <= step - q <= 3:
                continue
            for k in range(4):
                for s in range(2):
                    @pl.when((r != k) & (ring_dist(k, s) == step - q))
                    def _():
                        c_copy(k, s, q, c_held(k, s, q)).wait_recv()
                        if step - q < 3:
                            c_copy(k, s, q, c_held(k, s, q)).start()

    def corner_start():
        @pl.when(is_row_source)
        def _():
            for q in range(2):
                for s in range(2):
                    c_partner(s, q).start()
                    c_copy(r, s, q, c_from(s, q)).start()
            for s in range(2):
                c_own(s).start()

    def corner_swap():
        @pl.when(is_row_source)
        def _():
            for s in range(2):
                c_own(s).wait()

        for k in range(4):
            c_core(k).start()

    if free:
        todo = [(jj, d) for jj in range(4) for d in (1, 3, 2)]
        make_column_panel_free()
        swap_cores()
        arrange(0)
        z_send(0)
        cross(0, 0)
        make_row_panel_free()
        arrange(1)
        cross(1, 0)
        z_later = {1: 1, 2: 2, 3: 3}
    else:
        todo = [(0, g) for g in range(4)] + [(jj, 0) for jj in range(1, 4)]
        todo += [(jj, g) for jj in range(1, 4) for g in range(1, 4)]
        swap_cores()
        arrange(0)
        z_send(0)
        for jj in range(1, 4):
            arrange(jj)
            z_send_first(jj)
        for jj in range(1, 4):
            z_send_rest(jj)
        for item in todo[:7]:
            cross(*item)
        todo = todo[7:]
        own_waits()
        make_column_panel()
        make_row_panel()
        z_later = {}
    for slot in range(1, 7):
        column_slot(slot)
        for step in {4: (0,), 5: (1, 2), 6: (3, 4)}.get(slot, ()):
            corner_ring(step)
        if slot in z_later:
            z_send(z_later[slot])
        if free and slot == 1:
            arrange(2)
            cross(2, 0)
            arrange(3)
            cross(3, 0)
        if free and slot == 2:
            own_waits()
        if slot > 1:
            for item in todo[:2]:
                cross(*item)
            todo = todo[2:]
            row_ring(slot - 2)
    corner_swap()
    for item in todo:
        cross(*item)

    @pl.when(is_row_source)
    def _():
        own_u.wait()

    for k in range(4):
        c_core(k).wait()
    load_pinv.wait()
    factor_panels(r, c, CR, UR, pinv, Vh, Vl, frow, PB, U)
    out_copies = [
        pltpu.make_async_copy(src, dst, outs.at[i])
        for i, (src, dst) in enumerate(((Vh, Vh_out), (Vl, Vl_out), (frow, frow_out)))
    ]
    for copy in out_copies:
        copy.start()

    for jj in range(4):
        core_copy(jj).wait_send()
        for d in (1, 2, 3):
            z_copy(jj, d).wait_send()

    for item in queue[len(queue) - WINDOW:]:
        x_copy(*item).wait_send()
    for g in range(4):
        for jj in range(4):
            done = never
            if not free and jj == 0:
                done = is_row_source
            if not free and g == 0:
                done = done | is_col_source

            @pl.when(jnp.logical_not(done))
            def _():
                x_copy(jj, g).wait_recv()

    for copy in out_copies:
        copy.wait()

    @pl.when(is_row_source)
    def _():
        for q in range(2):
            for way in range(2):
                u_partner(way, q).wait_send()
                u_copy(r, way, q, PR.at[u_rows(way, q)]).wait_send()
                c_partner(way, q).wait_send()
                c_copy(r, way, q, c_from(way, q)).wait_send()
    for k in range(4):
        for way in range(2):
            dist = ring_dist(k, way)

            @pl.when((r != k) & (dist < 3))
            def _():
                for q in range(2):
                    u_copy(k, way, q, u_held(k, way, q)).wait_send()
                    c_copy(k, way, q, c_held(k, way, q)).wait_send()
    for s in range(2):
        for l in range(8):
            dist = (z + 4 - s) % 4 if l % 2 == 0 else (s + 4 - z) % 4
            cross_z = (s + shift[l]) % 4

            @pl.when(h == 0)
            def _():
                @pl.when(dist < 3)
                def _():
                    l_copy(s, l, LR.at[2 * s + core, l]).wait_send()

                @pl.when(z == cross_z)
                def _():
                    l_x(s, l).wait_send()

            @pl.when((h == 1) & (z == cross_z))
            def _():
                for d in (1, 3, 2):
                    l_three(s, l, d).wait_send()

            l_core(s, l).wait()


def split(a):
    hi = a.astype(bf16)
    return hi, (a - hi.astype(f32)).astype(bf16)


def dot3(a, b):
    ah, al = a
    bh, bl = b
    d = functools.partial(jnp.dot, preferred_element_type=f32)
    return d(ah, bh) + (d(ah, bl) + d(al, bh))


def factor_panels(r, c, CR, UR, pinv, Vh, Vl, frow, PB, U):
    for k in range(4):
        for j in range(4):
            PB[k * BS:(k + 1) * BS, j * BS:(j + 1) * BS] = CR[k, j % 2, j // 2]
        U[k * BS:(k + 1) * BS, :] = UR[k]
    for k in range(3):
        at, rest = k * BS, (k + 1) * BS
        lower = dot3(split(PB[rest:, at:rest]), split(pinv[k]))
        PB[rest:, at:rest] = lower
        low = split(lower)
        PB[rest:, rest:] = PB[rest:, rest:] - dot3(low, split(PB[at:rest, rest:]))
        U[rest:, :] = U[rest:, :] - dot3(low, split(U[at:rest, :]))

    @pl.when(r < 4)
    def _():
        rows = pl.ds(pl.multiple_of(r * BS, BS), BS)
        frow[...] = U[rows, :]

        @pl.when(c < 4)
        def _():
            frow[:, 0:BS] = PB[rows, pl.ds(pl.multiple_of(c * BS, BS), BS)]

    @pl.when(r >= 4)
    def _():
        frow[...] = jnp.zeros_like(frow)

    @pl.when(c < 4)
    def _():
        on = lax.broadcasted_iota(jnp.int32, (K * BS, BS), 0)
        across = lax.broadcasted_iota(jnp.int32, (K * BS, BS), 1)
        U[:, 0:BS] = jnp.where(on == across + c * BS, -1.0, 0.0).astype(f32)

    for m in range(3, -1, -1):
        at, rest = m * BS, (m + 1) * BS
        total = U[at:rest, :]
        if m < 3:
            total = total - dot3(split(PB[at:rest, rest:]), (Vh[rest:, :], Vl[rest:, :]))
        vh, vl = split(dot3(split(pinv[m]), split(total)))
        Vh[at:rest, :] = vh
        Vl[at:rest, :] = vl


def child_step(imap, pos, child, l):
    at = [local_row(imap, child, jj, pos[0]) for jj in range(4)]
    passed = sum((a <= l).astype(jnp.int32) for a in at)
    found = sum((a == l).astype(jnp.int32) for a in at)
    return jnp.clip(passed - 1, 0, 3), found


def update_kernel(imap, mask, pos, F, LRl, R, X, Vh, Vl, frow, out, ah, al):
    l = pl.program_id(0)
    r, c = pos[0], pos[1]
    h, z, core = c // 8, (c // 2) % 4, c % 2
    for p in range(4):
        hi, lo = split(LRl[p, 0])
        ah[:, p * BS:(p + 1) * BS] = hi
        al[:, p * BS:(p + 1) * BS] = lo
    children = []
    for child, source in ((h, R), (1 - h, X)):
        found = child_step(imap, pos, child, l)[1]
        children.append((source, found, [place(imap, child, g, h, z, core) for g in range(4)]))
    for lc in range(4):
        cols = slice(lc * BS, (lc + 1) * BS)
        total = F[:, cols]
        for source, found, places in children:
            group = jnp.int32(0)
            hit = jnp.int32(0)
            for g, (lands, at) in enumerate(places):
                here = (lands & (at == lc)).astype(jnp.int32) * found
                group = jnp.where(here > 0, g, group)
                hit = hit + here
            total = total + jnp.where(hit > 0, source[group, 0], 0.0)
        present = mask[r + 8 * l, c + 16 * lc].astype(f32)
        if lc == 0:
            present = present * (c >= 4).astype(f32)
        product = dot3((ah[...], al[...]), (Vh[:, cols], Vl[:, cols]))
        out[:, cols] = total * present - product

    @pl.when((l == 0) & (r < 4))
    def _():
        out[...] = frow[...]


def exchange(free, index_map, fill_mask, contrib, front, pivot_inverse):
    any_ = pl.BlockSpec(memory_space=pl.ANY)
    smem = pl.BlockSpec(memory_space=pltpu.SMEM)
    V = pltpu.VMEM
    dma = pltpu.SemaphoreType.DMA
    blk = (BS, BS)
    side = (4 * BS, 4 * BS)
    return pl.pallas_call(
        functools.partial(exchange_kernel, free),
        out_shape=[
            jax.ShapeDtypeStruct((4, 4) + blk, f32),
            jax.ShapeDtypeStruct((4, 4) + blk, f32),
            jax.ShapeDtypeStruct((4, 8) + blk, f32),
            jax.ShapeDtypeStruct(side, bf16),
            jax.ShapeDtypeStruct(side, bf16),
            jax.ShapeDtypeStruct((BS, 4 * BS), f32),
        ],
        in_specs=[smem, smem, any_, any_, any_],
        out_specs=[any_] * 6,
        scratch_shapes=[
            V((4, BS, 4 * BS), f32), V((4, 2, 2) + blk, f32), V(side, f32), V(side, f32),
            V((4,) + blk, f32), V(side, bf16), V(side, bf16), V((BS, 4 * BS), f32),
            dma((1,)), dma((3,)),
            V((4, BS, 4 * BS), f32), V((4, 2) + blk, f32),
            V((4,) + blk, f32), V((4,) + blk, f32), V((4,) + blk, f32), V((4,) + blk, f32),
            V((4, 4) + blk, f32), V((8,) + blk, f32), V((BS, 4 * BS), f32),
            V((8 * BS, BS), f32), V((BS, 4 * BS), f32),
            V((2, 4) + blk, f32), V((2, 4) + blk, f32),
            dma((4,)), dma((2,)), dma((4,)), dma((4,)), dma((4, 4)), dma((4, 4)), dma((4, 4)),
            dma((4, 4)), dma((4,)),
            dma((2, 4)), dma((2,)), dma((1,)), dma((2, 8)), dma((2, 8)), dma((2, 8)), dma((2, 8)),
            dma((2, 8)), dma((2, 8, 4)),
            dma((4, 2, 2)), dma((4, 2, 2)), dma((2, 2)), dma((1,)), dma((4, 2, 2)), dma((4, 2, 2)),
            dma((2, 2)), dma((2,)), dma((4,)), dma((4,)),
        ],
        compiler_params=pltpu.CompilerParams(
            collective_id=int(free), has_side_effects=True, vmem_limit_bytes=60 * 2**20
        ),
        name="exchange_%d" % free,
    )(index_map, fill_mask, contrib, front, pivot_inverse)


def body(front, contrib, pivot_inverse, index_map, fill_mask):
    pos = jnp.stack([lax.axis_index("row"), lax.axis_index("col")]).astype(jnp.int32)
    R, X, LR, Vh, Vl, frow = lax.cond(
        jnp.min(index_map[:, 0]) >= 4,
        functools.partial(exchange, True), functools.partial(exchange, False),
        index_map, fill_mask, contrib, front, pivot_inverse,
    )
    blk = (BS, BS)
    side = (4 * BS, 4 * BS)
    V = pltpu.VMEM

    def child_spec(own):
        def index(l, imap, mask, pos):
            child = pos[1] // 8
            if not own:
                child = 1 - child
            return 0, child_step(imap, pos, child, l)[0], 0, 0

        return pl.BlockSpec((4, 1) + blk, index)

    return pl.pallas_call(
        update_kernel,
        out_shape=jax.ShapeDtypeStruct(front.shape, f32),
        grid_spec=pltpu.PrefetchScalarGridSpec(
            num_scalar_prefetch=3,
            grid=(8,),
            in_specs=[
                pl.BlockSpec((BS, 4 * BS), lambda l, *_: (l, 0)),
                pl.BlockSpec((4, 1) + blk, lambda l, *_: (0, l, 0, 0)),
                child_spec(True),
                child_spec(False),
                pl.BlockSpec(side, lambda l, *_: (0, 0)),
                pl.BlockSpec(side, lambda l, *_: (0, 0)),
                pl.BlockSpec((BS, 4 * BS), lambda l, *_: (0, 0)),
            ],
            out_specs=pl.BlockSpec((BS, 4 * BS), lambda l, *_: (l, 0)),
            scratch_shapes=[V((BS, 4 * BS), bf16), V((BS, 4 * BS), bf16)],
        ),
        compiler_params=pltpu.CompilerParams(vmem_limit_bytes=60 * 2**20),
        name="update",
    )(index_map, fill_mask, pos, front, LR, R, X, Vh, Vl, frow)


def solution(mesh):
    in_specs = (P("row", "col"), P("row", "col"), P(), P(), P())
    out_specs = P("row", "col")
    return jax.shard_map(body, mesh=mesh, in_specs=in_specs, out_specs=out_specs, check_vma=False)
```

profile of v0, /device:TPU:118, one launch (start us, length us, event | category | flops | bytes accessed | tf_op | source)
XLA Modules:
  0.0 193.7 jit_solution(797116541895159093)
XLA Ops:
  0.0 1.3 slice_reduce_fusion
  2.0 167.0 %conditional.1 = ((f32[4,4,256,256]{3,2,1,0:T(8,128)}, f32[4,4,256,256]{3,2,1,0:T(8,128)}, f32[4,8,256,256]{3,2,1,0:T(8,128)}, bf16[1024,1024]{1,0:T(8,128)(2,1)...) conditional(s32[]{:T(128)} %convert_element_type.3, (s32[2,32]{1,0:T(2,128)}, s32[64,64]{1,0:T(8,128)}, ...), branch_computations={%region_1.0_spmd, %region_2.0_spmd} | conditional | bytes 8 | solution.py:747
  2.2 166.5 %exchange_1.1 = (f32[4,4,256,256]{3,2,1,0:T(8,128)}, f32[4,4,256,256]{3,2,1,0:T(8,128)}, f32[4,8,256,256]{3,2,1,0:T(8,128)}, bf16[1024,1024]{1,0:T(8,128)(2,1)S(...) custom-call(s32[2,32]{1,0:T(2,128)} %get-tuple-element.30.imap, s32[64,64]{1,0:T(8,128)} %get-tuple-element.31.mask, ...), custom_call_target="tpu_custom_call" | custom-call | tf_op jit(solution)/shard_map/cond/branch_1_fun/exchange_1/pallas_call | solution.py:710
  169.0 0.6 pad_add_fusion.pos
  169.6 24.1 %update.1 = f32[2048,1024]{1,0:T(8,128)} custom-call(s32[2,32]{1,0:T(2,128)} %imap.1, s32[64,64]{1,0:T(8,128)} %mask.1, s32[2]{0:T(128)} %pad_add_fusion.pos, f32[2048,1024]{1,0:T(8,128)} %F.1, f32[4,8,256,256]{3,2,1,0:T(8,128)} %get-tuple-element.41.LRl, f32[4,4,256,256]{3,2,1,0:T(8,128)} %get-tuple-element.42.R, f32[4,4,256,256]{3,2,1,0:T(8,128)} %get-tuple-element.43.X, ...), custom_call_target="tpu_custom_call" | custom-call | tf_op jit(solution)/shard_map/update/pallas_call | solution.py:765
where the time goes:
time: 194 us
  Pallas kernels  191 us (98%)
    pallas_call x1, Pallas kernels, exchange(): pl.pallas_call(functools.partial(exchange_kernel, free), out_shape=[jax.S...  166 us
    pallas_call x1, Pallas kernels, body(): pl.pallas_call(update_kernel, out_shape=jax.ShapeDtypeStruct(front.shape,...  24.1 us

commit v1 on v0

--- a/solution.py
+++ b/solution.py
@@ -427,8 +427,9 @@
             LR.at[2 * s + core, 0], CR.at[jnp.minimum(r, 3), core, s], ccopy.at[s]
         )
 
-    def c_core(k):
-        return remote(CR.at[k, core], CR.at[k, core], Ccs.at[k], Ccr.at[k], core_peer)
+    def c_core(k, s, q):
+        held = c_held(k, s, q)
+        return remote(held, held, Ccs.at[k, s, q], Ccr.at[k, s, q], core_peer)
 
     def ring_dist(k, way):
         s = k // 2
@@ -457,6 +458,7 @@
                         c_copy(k, s, q, c_held(k, s, q)).wait_recv()
                         if step - q < 3:
                             c_copy(k, s, q, c_held(k, s, q)).start()
+                        c_core(k, s, q).start()
 
     def corner_start():
         @pl.when(is_row_source)
@@ -473,9 +475,8 @@
         def _():
             for s in range(2):
                 c_own(s).wait()
-
-        for k in range(4):
-            c_core(k).start()
+                for q in range(2):
+                    c_core(r, s, q).start()
 
     if free:
         todo = [(jj, d) for jj in range(4) for d in (1, 3, 2)]
@@ -519,12 +520,13 @@
             cross(3, 0)
         if free and slot == 2:
             own_waits()
+        if slot == 5:
+            corner_swap()
         if slot > 1:
             for item in todo[:2]:
                 cross(*item)
             todo = todo[2:]
             row_ring(slot - 2)
-    corner_swap()
     for item in todo:
         cross(*item)
 
@@ -533,7 +535,9 @@
         own_u.wait()
 
     for k in range(4):
-        c_core(k).wait()
+        for s in range(2):
+            for q in range(2):
+                c_core(k, s, q).wait()
     load_pinv.wait()
     factor_panels(r, c, CR, UR, pinv, Vh, Vl, frow, PB, U)
     out_copies = [
@@ -733,7 +737,7 @@
             dma((2, 4)), dma((2,)), dma((1,)), dma((2, 8)), dma((2, 8)), dma((2, 8)), dma((2, 8)),
             dma((2, 8)), dma((2, 8, 4)),
             dma((4, 2, 2)), dma((4, 2, 2)), dma((2, 2)), dma((1,)), dma((4, 2, 2)), dma((4, 2, 2)),
-            dma((2, 2)), dma((2,)), dma((4,)), dma((4,)),
+            dma((2, 2)), dma((2,)), dma((4, 2, 2)), dma((4, 2, 2)),
         ],
         compiler_params=pltpu.CompilerParams(
             collective_id=int(free), has_side_effects=True, vmem_limit_bytes=60 * 2**20

time: 194 us -> 194 us (level)
  no operation moved by 1% of the time
where the time goes in v1:
time: 194 us
  Pallas kernels  191 us (98%)
    pallas_call x1, Pallas kernels, exchange(): pl.pallas_call(functools.partial(exchange_kernel, free), out_shape=[jax.S...  167 us
    pallas_call x1, Pallas kernels, body(): pl.pallas_call(update_kernel, out_shape=jax.ShapeDtypeStruct(front.shape,...  24.1 us

profile of v1, /device:TPU:118, one launch (start us, length us, event | category | flops | bytes accessed | tf_op | source)
XLA Modules:
  0.0 193.9 jit_solution(18247706311903504423)
XLA Ops:
  0.0 1.3 slice_reduce_fusion
  2.0 167.2 %conditional.1 = ((f32[4,4,256,256]{3,2,1,0:T(8,128)}, f32[4,4,256,256]{3,2,1,0:T(8,128)}, f32[4,8,256,256]{3,2,1,0:T(8,128)}, bf16[1024,1024]{1,0:T(8,128)(2,1)...) conditional(s32[]{:T(128)} %convert_element_type.3, (s32[2,32]{1,0:T(2,128)}, s32[64,64]{1,0:T(8,128)}, ...), branch_computations={%region_1.0_spmd, %region_2.0_spmd} | conditional | bytes 8 | solution.py:751
  2.2 166.7 %exchange_1.1 = (f32[4,4,256,256]{3,2,1,0:T(8,128)}, f32[4,4,256,256]{3,2,1,0:T(8,128)}, f32[4,8,256,256]{3,2,1,0:T(8,128)}, bf16[1024,1024]{1,0:T(8,128)(2,1)S(...) custom-call(s32[2,32]{1,0:T(2,128)} %get-tuple-element.30.imap, s32[64,64]{1,0:T(8,128)} %get-tuple-element.31.mask, ...), custom_call_target="tpu_custom_call" | custom-call | tf_op jit(solution)/shard_map/cond/branch_1_fun/exchange_1/pallas_call | solution.py:714
  169.2 0.6 pad_add_fusion.pos
  169.8 24.1 %update.1 = f32[2048,1024]{1,0:T(8,128)} custom-call(s32[2,32]{1,0:T(2,128)} %imap.1, s32[64,64]{1,0:T(8,128)} %mask.1, s32[2]{0:T(128)} %pad_add_fusion.pos, f32[2048,1024]{1,0:T(8,128)} %F.1, f32[4,8,256,256]{3,2,1,0:T(8,128)} %get-tuple-element.41.LRl, f32[4,4,256,256]{3,2,1,0:T(8,128)} %get-tuple-element.42.R, f32[4,4,256,256]{3,2,1,0:T(8,128)} %get-tuple-element.43.X, ...), custom_call_target="tpu_custom_call" | custom-call | tf_op jit(solution)/shard_map/update/pallas_call | solution.py:769
